TPU v7x, 32 devices: a whole 2x2x4 slice. The times are simulated.
32 devices in a mesh: rows: 4 (over y, x), cols: 8 (over z, core).
Axes of the slice: x: 2, y: 2, z: 4, core: 2. Of those that a mesh axis runs over, the one named last changes fastest.
Arguments:
- ancestor_inv: bfloat16 [4096, 4096], P('rows', 'cols'), may hold values from -0.125 to 0.125
- lfactor: bfloat16 [8, 256, 6, 256], P('cols'), may hold values from -0.8984375 to 0.8984375
- struct: int32 [6, 8], replicated, may hold values from 0 to 15, as said below
- validity: int32 [6, 8], replicated, may hold values from 0 to 1, as said below
- diag_inverse: float32 [6, 256, 256], replicated, may hold values from -6 to 6
Outputs:
- column_block: bfloat16 [4096, 1536], P(('rows', 'cols'))
- diagonal_block: float32 [6, 256, 256], replicated
Inputs may be any that keep to these rules, and one draw needn't show every extreme that they name: `struct`: within a supernode the 8 tile indices are distinct and increasing, and every list holds tiles 0 and 15. `validity`: every tile index of 0 to 15 is a valid entry of some supernode's list; some supernode has all 8 flags set.
All inputs are finite; a program needn't handle non-finite values.
Results may differ from a plain program's by a relative error of at most 0.001.
Values may be sent and summed in bfloat16 or wider, within the bound.
A program may use at most 192 MiB of HBM per device.

v0:
```python
import jax
import jax.numpy as jnp
from jax import lax
from jax.sharding import PartitionSpec as P


def choose_tiles(tile_lists, flag_lists, first_tile, tile_count):
    wanted = first_tile + jnp.arange(tile_count, dtype=jnp.int32)
    hits = (tile_lists[:, :, None] == wanted[None, None, :]) & (flag_lists[:, :, None] > 0)
    return hits.astype(jnp.bfloat16)


def body(ancestor_inv, lfactor, struct, validity, diag_inverse):
    row_extent, col_extent = ancestor_inv.shape
    tile_size = lfactor.shape[1]
    super_count = lfactor.shape[2]
    col_tiles = col_extent // tile_size
    slab_rows = row_extent // lax.axis_size("cols")
    row_index = lax.axis_index("rows")
    col_index = lax.axis_index("cols")
    col_first = col_index * col_tiles
    global_start = row_index * row_extent + col_index * slab_rows
    own_tile = global_start // tile_size
    offset = global_start % tile_size
    front_groups = (0, super_count)
    first_node, members = front_groups
    shard_piece = lax.all_gather(lfactor, "cols", axis=0, tiled=True)
    picker = choose_tiles(struct, validity, col_first, col_tiles)
    col_acc = jnp.einsum(
        "kpt,pakb->takb", picker, shard_piece, preferred_element_type=jnp.float32
    ).astype(jnp.bfloat16)
    nearby = choose_tiles(struct, validity, own_tile, 1)[:, :, 0]
    slab_piece = lax.dynamic_slice_in_dim(shard_piece, offset, slab_rows, 1)
    row_acc = jnp.einsum("kp,pakb->akb", nearby, slab_piece, preferred_element_type=jnp.float32)
    right_side = col_acc.reshape(col_extent, members * tile_size)
    block_rows = ancestor_inv
    summed_rows = lax.psum_scatter(
        -jnp.dot(block_rows, right_side, preferred_element_type=jnp.float32),
        "cols",
        scatter_dimension=0,
        tiled=True,
    )
    updates = summed_rows.reshape(slab_rows, members, tile_size)
    partial_value = jnp.einsum("akb,akc->kbc", row_acc, updates, precision=lax.Precision.HIGHEST)
    diagonal_sum = lax.psum(partial_value, ("rows", "cols"))
    present = jnp.max(choose_tiles(struct, validity, own_tile, 1)[:, :, 0], axis=1).astype(
        jnp.float32
    )
    block_rows = (updates * present[None, :, None]).astype(jnp.bfloat16)
    diagonal = diag_inverse - diagonal_sum
    block_rows, diagonal = (block_rows, diagonal)
    column_block = block_rows.reshape(slab_rows, super_count * tile_size)
    return (column_block, diagonal)


def solution(mesh):
    return jax.shard_map(
        body,
        mesh=mesh,
        in_specs=(P("rows", "cols"), P("cols", None, None, None), P(), P(), P()),
        out_specs=(P(("rows", "cols"), None), P()),
        check_vma=False,
    )
```

profile of v0, /device:TPU:0, one launch (start us, length us, event | category | flops | bytes accessed | tf_op | source)
XLA Modules:
  0.0 310.0 jit_solution(547342799482646173)
XLA Ops:
  7.2 0.0 copy-start
  7.2 0.0 all-gather.2.cloned.1.call-start
  7.2 0.7 all-gather.2.cloned.1.call-update
  7.9 0.0 reduce-scatter.2.cloned.1.call-start
  8.0 0.8 convert_reduce_fusion
  8.8 68.3 %all-gather.2.cloned.1.call-done = bf16[8,256,6,256]{3,1,2,0:T(8,128)(2,1)} async-done(((bf16[1,256,6,256]{3,1,2,0:T(8,128)(2,1)}), bf16[8,256,6,256]{3,1,2,0:T(8,128)(2,1)}) %all-gather.2.cloned.1.call-update) | async-done | bytes 6291472 | tf_op jit(solution)/shard_map/all_gather | solution.py:27
  77.1 8.1 %fusion.7 = bf16[2,256,6,256]{3,0,1,2:T(2,128)(2,1)} fusion(bf16[8,256,6,256]{3,1,2,0:T(8,128)(2,1)} %all-gather.2.cloned.1.call-done, pred[6,8]{1,0:T(8,128)(4,1)S(1)} %get-tuple-element.10, s32[6,8]{1,0:T(8,128)} %param.7, s32[2]{0:T(128)S(1)} %iota_add_fusion), kind=kOutput, calls=%fused_computation.6 | convolution fusion | flops 13369536 | bytes 7864568 | tf_op jit(solution)/shard_map/kpt,pakb->takb/dot_general | solution.py:29
  85.2 5.2 %copy.15 = bf16[2,256,6,256]{1,0,3,2:T(2,128)(2,1)S(1)} copy(bf16[2,256,6,256]{3,0,1,2:T(2,128)(2,1)} %fusion.7) | data formatting | bytes 3145728 | tf_op jit(solution)/shard_map/convert_element_type | solution.py:31
  90.5 0.3 copy.23
  90.8 0.0 copy-done
  90.8 4.5 %negate_bitcast_fusion = f32[1024,1536]{0,1:T(8,128)} fusion(bf16[512,1536]{0,1:T(8,128)(2,1)S(1)} %bitcast.26, bf16[1024,512]{1,0:T(8,128)(2,1)S(1)} %copy-done), kind=kOutput, calls=%fused_computation.2 | convolution fusion | flops 1612185600 | bytes 8912896 | tf_op jit(solution)/shard_map/dot_general | solution.py:38
  95.3 0.0 reduce-scatter.2.cloned.1.call-update
  95.3 0.2 all-reduce.2.cloned.1.call-start
  95.6 3.7 %constant_dynamic-slice_fusion = bf16[8,128,6,256]{3,1,2,0:T(8,128)(2,1)S(1)} fusion(bf16[8,256,6,256]{3,1,2,0:T(8,128)(2,1)} %all-gather.2.cloned.1.call-done, s32[]{:T(128)S(6)} %select_n.16), kind=kLoop, calls=%fused_computation.21 | loop fusion | bytes 6291460 | tf_op jit(solution)/shard_map/dynamic_slice | solution.py:33
  99.2 2.1 fusion.2
  101.3 0.5 copy.21
  101.8 62.1 %reduce-scatter.2.cloned.1.call-done = f32[128,1536]{0,1:T(8,128)} async-done(((f32[1024,1536]{0,1:T(8,128)}), f32[128,1536]{0,1:T(8,128)}) %reduce-scatter.2.cloned.1.call-update) | async-done | bytes 786448 | tf_op jit(solution)/shard_map/reduce_scatter | solution.py:37
  163.9 0.0 copy-start.1
  163.9 3.8 %fusion.10 = f32[6,256,256]{2,1,0:T(8,128)} fusion(f32[128,6,256]{0,2,1:T(8,128)} %bitcast.25, f32[6,1,128,256]{2,3,0,1:T(8,128)S(1)} %copy.21), kind=kOutput, calls=%fused_computation.7 | convolution fusion | flops 603979776 | bytes 3145728 | tf_op jit(solution)/shard_map/akb,akc->kbc/dot_general | solution.py:44
  167.7 0.0 all-reduce.2.cloned.1.call-update
  167.7 0.1 mul.25
  167.8 0.0 copy-done.1
  167.8 0.3 multiply_convert_fusion
  168.1 0.9 copy.17
  169.0 131.2 %all-reduce.2.cloned.1.call-done = f32[6,256,256]{2,1,0:T(8,128)} async-done(((f32[6,256,256]{2,1,0:T(8,128)}), f32[6,256,256]{2,1,0:T(8,128)}) %all-reduce.2.cloned.1.call-update) | async-done | bytes 1572880 | tf_op jit(solution)/shard_map/psum | solution.py:45
  300.2 3.2 %sub.8 = f32[6,256,256]{2,1,0:T(8,128)} subtract(f32[6,256,256]{2,1,0:T(8,128)} %param.9, f32[6,256,256]{2,1,0:T(8,128)} %all-reduce.2.cloned.1.call-done) | non-fusion elementwise | flops 393216 | bytes 4718592 | tf_op jit(solution)/shard_map/sub | solution.py:50
  (2 shorter events, 0.0 us)
Async XLA Ops:
  7.2 83.6 %copy-start = (bf16[1024,512]{1,0:T(8,128)(2,1)S(1)}, bf16[1024,512]{1,0:T(8,128)(2,1)}, u32[]{:S(2)}) copy-start(bf16[1024,512]{1,0:T(8,128)(2,1)} %param.5) | copy-start | bytes 3145732
  7.2 70.0 %all-gather.2.cloned.1.call-start = ((), (), s32[]{:S(2)}) async-start(), calls=%async_computation.1 | async-start | bytes 7077888 | tf_op jit(solution)/shard_map/all_gather | solution.py:27
  7.9 156.0 %reduce-scatter.2.cloned.1.call-start = ((), (), s32[]{:S(2)}) async-start(), calls=%async_computation.2 | async-start | bytes 7077888 | tf_op jit(solution)/shard_map/reduce_scatter | solution.py:37
  95.3 204.9 %all-reduce.2.cloned.1.call-start = ((), (), s32[]{:S(2)}) async-start(), calls=%async_computation.3 | async-start | bytes 3145728 | tf_op jit(solution)/shard_map/psum | solution.py:45
  163.9 3.9 %copy-start.1 = (f32[128,1536]{0,1:T(8,128)S(1)}, f32[128,1536]{0,1:T(8,128)}, u32[]{:S(2)}) copy-start(f32[128,1536]{0,1:T(8,128)} %reduce-scatter.2.cloned.1.call-done) | copy-start | bytes 2359300
Sparse Core Ops, SparseCore 0:
  9.7 67.4 all-gather.1
  95.4 68.4 reduce-scatter.1
  169.8 130.3 all-reduce.1
where the time goes:
time: 310 us
  waiting for transfers between devices  262 us (85%)
  matrix products  18.4 us (6%)
  between operations  13.8 us (4%)
  local copies, waits for them, and re-layouts  10.7 us (3%)
  other arithmetic  4.32 us (1%)
    psum x1, waiting for transfers between devices, body(): diagonal_sum = lax.psum(partial_value, ('rows', 'cols'))  131 us
    all_gather x1, waiting for transfers between devices, body(): shard_piece = lax.all_gather(lfactor, 'cols', axis=0, tiled=True)  68.3 us
    reduce_scatter x1, waiting for transfers between devices, body(): lax.psum_scatter(-jnp.dot(block_rows, right_side, preferred_element_type=...  62.1 us
    dot_general x1, matrix products, body(): jnp.einsum('kpt,pakb->takb', picker, shard_piece, preferred_element_type=...  8.09 us
  transfers between devices with their start and end apart: 3, of which 3 were waited for; matrix products, arithmetic and copies ran while one was open for 3% of the time, Pallas kernels for 0%

commit v1 on v0

v1 whole, which is shorter than its diff:
```python
import functools

import jax
import jax.numpy as jnp
from jax import lax
from jax.experimental import pallas as pl
from jax.experimental.pallas import tpu as pltpu
from jax.sharding import PartitionSpec as P

MESH = pl.DeviceIdType.MESH


def kernel(
    R, C, a_ref, l_ref, struct_ref, valid_ref, d_ref, col_ref, diag_ref,
    abuf, lbuf, q, x1, x2, x3, f,
    loc_sem, a_send, a_recv,
    lz_send_up, lz_send_dn, lz_recv, lp_send, lp_recv, lc_send, lc_recv, lo_send, lo_recv,
    d1_send, d1_recv, d2_send, d2_recv, d3_send, d3_recv,
    d4_send, d4_recv, d5_send, d5_recv, d6_send, d6_recv,
):
    Z = C // 2
    r = lax.axis_index("rows")
    c = lax.axis_index("cols")
    z = c // 2
    core = c % 2
    sib = z * 2 + 1 - core
    E, K, S = l_ref.shape[0], l_ref.shape[1], l_ref.shape[2]
    NP = C * E
    TPD = a_ref.shape[1] // S
    M = a_ref.shape[0] // C
    piece = S // R

    def wrap(v, n):
        return lax.rem(v, n)

    barrier = pltpu.get_barrier_semaphore()
    for d in range(1, C):
        pl.semaphore_signal(barrier, inc=1, device_id=(r, wrap(c + d, C)), device_id_type=MESH)
    for d in range(1, R):
        pl.semaphore_signal(barrier, inc=1, device_id=(wrap(r + d, R), c), device_id_type=MESH)
    pl.semaphore_wait(barrier, C - 1 + R - 1)

    def remote(src, dst, ssem, rsem, dev):
        return pltpu.make_async_remote_copy(
            src_ref=src, dst_ref=dst, send_sem=ssem, recv_sem=rsem,
            device_id=dev, device_id_type=MESH,
        )

    def entry(zz):
        return zz * 2 + core

    def rows_of(rr):
        return pl.ds(pl.multiple_of(rr * piece, piece), piece)

    def own_z(zn, ssem):
        return remote(
            l_ref.at[:, :, rows_of(r), :], lbuf.at[c, :, :, rows_of(r), :],
            ssem, lz_recv.at[z], (r, entry(zn)),
        )

    @pl.when(z + 1 < Z)
    def _():
        own_z(z + 1, lz_send_up.at[z]).start()

    @pl.when(z > 0)
    def _():
        own_z(z - 1, lz_send_dn.at[z]).start()

    own_core = remote(l_ref, lbuf.at[c], lo_send, lo_recv, (r, sib))
    own_core.start()
    own_l = pltpu.make_async_copy(l_ref, lbuf.at[c], loc_sem.at[0])
    own_l.start()

    def a_copy(d, j):
        cn = wrap(c + d, C)
        return remote(
            a_ref.at[pl.ds(pl.multiple_of(cn * M, M), M), pl.ds(j * S, S)],
            abuf.at[c * TPD + j], a_send.at[d, j], a_recv.at[d, j], (r, cn),
        )

    for d in range(1, C):
        for j in range(TPD):
            a_copy(d, j).start()
    own_a = []
    for j in range(TPD):
        own_a.append(pltpu.make_async_copy(
            a_ref.at[pl.ds(pl.multiple_of(c * M, M), M), pl.ds(j * S, S)],
            abuf.at[c * TPD + j], loc_sem.at[1 + j],
        ))
        own_a[-1].start()

    def fwd_z(zz, zn, ssem):
        ref = lbuf.at[entry(zz), :, :, rows_of(r), :]
        return remote(ref, ref, ssem, lz_recv.at[zz], (r, entry(zn)))

    def plane(zz, rr, rn):
        ref = lbuf.at[entry(zz), :, :, rows_of(rr), :]
        return remote(ref, ref, lp_send.at[zz, rn], lp_recv.at[zz, rr], (rn, c))

    def across(zz, rr):
        ref = lbuf.at[entry(zz), :, :, rows_of(rr), :]
        return remote(ref, ref, lc_send.at[zz, rr], lc_recv.at[zz, rr], (r, sib))

    def across_in(zz, rr):
        ref = lbuf.at[zz * 2 + 1 - core, :, :, rows_of(rr), :]
        return remote(ref, ref, lc_send.at[zz, rr], lc_recv.at[zz, rr], (r, sib))

    def arrived(zz):
        for d in range(1, R):
            plane(zz, r, wrap(r + d, R)).start()
        across(zz, r).start()

    for s in range(1, Z):
        @pl.when(z - s >= 0)
        def _():
            fwd_z(z - s, z, lz_send_up.at[z - s]).wait_recv()

            @pl.when(z + 1 < Z)
            def _():
                fwd_z(z - s, z + 1, lz_send_up.at[z - s]).start()
            arrived(z - s)

        @pl.when(z + s < Z)
        def _():
            fwd_z(z + s, z, lz_send_dn.at[z + s]).wait_recv()

            @pl.when(z > 0)
            def _():
                fwd_z(z + s, z - 1, lz_send_dn.at[z + s]).start()
            arrived(z + s)

    for s in range(1, Z):
        zz = wrap(z + s, Z)
        for d in range(1, R):
            rr = wrap(r + d, R)
            plane(zz, rr, r).wait_recv()
            across(zz, rr).start()

    own_l.wait()
    remote(l_ref, lbuf.at[sib], lo_send, lo_recv, (r, sib)).wait_recv()
    for cp in own_a:
        cp.wait()
    for d in range(1, C):
        cs = wrap(c + C - d, C)
        for j in range(TPD):
            remote(
                abuf.at[cs * TPD + j], abuf.at[cs * TPD + j],
                a_send.at[d, j], a_recv.at[d, j], (r, cs),
            ).wait_recv()
    for s in range(1, Z):
        for d in range(R):
            across_in(wrap(z + s, Z), wrap(r + d, R)).wait_recv()

    start_row = r * (C * M) + c * M
    own_tile = start_row // S
    offset = pl.multiple_of(start_row % S, M)

    def one_node(k, carry):
        acc = jnp.zeros((M, S), jnp.float32)
        present = jnp.int32(0)
        which = jnp.int32(0)
        for p in range(NP):
            t = struct_ref[k, p]
            ok = valid_ref[k, p] > 0
            hit = jnp.where(ok & (t == own_tile), 1, 0)
            present = present + hit
            which = which + hit * p
            term = jnp.dot(
                abuf[t], lbuf[p // E, p % E, k], preferred_element_type=jnp.float32
            )
            acc = acc + term * jnp.where(ok, 1.0, 0.0)
        here = present.astype(jnp.float32)
        col_ref[:, pl.ds(pl.multiple_of(k * S, S), S)] = (acc * (-here)).astype(jnp.bfloat16)
        panel = lbuf[which // E, which % E, k, pl.ds(offset, M), :] * here.astype(jnp.bfloat16)
        hi = acc.astype(jnp.bfloat16)
        lo = (acc - hi.astype(jnp.float32)).astype(jnp.bfloat16)
        out = lax.dot_general(
            jnp.concatenate([panel, panel], axis=0), jnp.concatenate([hi, lo], axis=0),
            (((0,), (0,)), ((), ())), preferred_element_type=jnp.float32,
        )
        at = pl.ds(pl.multiple_of(k * S, S), S)
        q[0, at, :] = out[:, : S // 2]
        q[1, at, :] = out[:, S // 2 :]
        return carry

    lax.fori_loop(0, K, one_node, 0)

    n_r = (K * S) // R
    n_z = n_r // Z

    def at_r(rr):
        return pl.ds(pl.multiple_of(rr * n_r, n_r), n_r)

    def at_z(rr, zz):
        return pl.ds(pl.multiple_of(rr * n_r + zz * n_z, n_z), n_z)

    d1 = remote(q.at[1 - core], x1, d1_send, d1_recv, (r, sib))
    d1.start()
    d1.wait_recv()
    x1[...] = x1[...] + q[core]
    d2 = []
    for d in range(1, R):
        rn = wrap(r + d, R)
        d2.append(remote(x1.at[at_r(rn)], x2.at[d - 1], d2_send.at[d - 1], d2_recv.at[d - 1], (rn, c)))
        d2[-1].start()
    part = x1[at_r(r), :]
    for d in range(1, R):
        d2[d - 1].wait_recv()
        part = part + x2[d - 1]
    q[core, at_r(0), :] = part
    d3 = []
    for s in range(1, Z):
        zn = wrap(z + s, Z)
        d3.append(remote(
            q.at[core, at_z(0, zn)], x3.at[s - 1], d3_send.at[s - 1], d3_recv.at[s - 1],
            (r, entry(zn)),
        ))
        d3[-1].start()
    part = q[core, at_z(0, z), :]
    for s in range(1, Z):
        d3[s - 1].wait_recv()
        part = part + x3[s - 1]
    f[core, at_z(r, z), :] = part
    d4 = []
    for s in range(1, Z):
        ref = f.at[core, at_z(r, z)]
        d4.append(remote(ref, ref, d4_send.at[s - 1], d4_recv.at[s - 1], (r, entry(wrap(z + s, Z)))))
        d4[-1].start()
    for s in range(1, Z):
        ref = f.at[core, at_z(r, wrap(z + Z - s, Z))]
        remote(ref, ref, d4_send.at[s - 1], d4_recv.at[s - 1], (r, c)).wait_recv()
    d5 = []
    for d in range(1, R):
        ref = f.at[core, at_r(r)]
        d5.append(remote(ref, ref, d5_send.at[d - 1], d5_recv.at[d - 1], (wrap(r + d, R), c)))
        d5[-1].start()
    d6 = []
    ref = f.at[core, at_r(r)]
    d6.append(remote(ref, ref, d6_send.at[0], d6_recv.at[0], (r, sib)))
    d6[-1].start()
    for d in range(1, R):
        ref = f.at[core, at_r(wrap(r + R - d, R))]
        remote(ref, ref, d5_send.at[d - 1], d5_recv.at[d - 1], (r, c)).wait_recv()
        d6.append(remote(ref, ref, d6_send.at[d], d6_recv.at[d], (r, sib)))
        d6[-1].start()
    for d in range(R):
        ref = f.at[1 - core, at_r(wrap(r + R - d, R))]
        remote(ref, ref, d6_send.at[d], d6_recv.at[d], (r, sib)).wait_recv()
    for k in range(K):
        for h in range(2):
            cut = slice(h * (S // 2), (h + 1) * (S // 2))
            diag_ref[k, :, cut] = d_ref[k, :, cut] + f[h, k * S : (k + 1) * S, :]

    @pl.when(z + 1 < Z)
    def _():
        own_z(z + 1, lz_send_up.at[z]).wait_send()

    @pl.when(z > 0)
    def _():
        own_z(z - 1, lz_send_dn.at[z]).wait_send()

    own_core.wait_send()
    for d in range(1, C):
        for j in range(TPD):
            a_copy(d, j).wait_send()

    def sent(zz):
        for d in range(1, R):
            plane(zz, r, wrap(r + d, R)).wait_send()
        across(zz, r).wait_send()

    for s in range(1, Z):
        @pl.when(z - s >= 0)
        def _():
            @pl.when(z + 1 < Z)
            def _():
                fwd_z(z - s, z + 1, lz_send_up.at[z - s]).wait_send()
            sent(z - s)

        @pl.when(z + s < Z)
        def _():
            @pl.when(z > 0)
            def _():
                fwd_z(z + s, z - 1, lz_send_dn.at[z + s]).wait_send()
            sent(z + s)

    for s in range(1, Z):
        zz = wrap(z + s, Z)
        for d in range(1, R):
            across(zz, wrap(r + d, R)).wait_send()
    for cp in [d1] + d2 + d3 + d4 + d5 + d6:
        cp.wait_send()


def body(R, C, ancestor_inv, lfactor, struct, validity, diag_inverse):
    E, S, K, _ = lfactor.shape
    Z = C // 2
    rows, width = ancestor_inv.shape
    M = rows // C
    TPD = width // S
    NT = C * TPD
    tall = K * S
    half = S // 2
    factor = jnp.transpose(lfactor, (0, 2, 1, 3))
    dma = pltpu.SemaphoreType.DMA
    column_block, diagonal = pl.pallas_call(
        functools.partial(kernel, R, C),
        out_shape=(
            jax.ShapeDtypeStruct((M, K * S), jnp.bfloat16),
            jax.ShapeDtypeStruct((K, S, S), jnp.float32),
        ),
        in_specs=[
            pl.BlockSpec(memory_space=pl.ANY),
            pl.BlockSpec(memory_space=pl.ANY),
            pl.BlockSpec(memory_space=pltpu.SMEM),
            pl.BlockSpec(memory_space=pltpu.SMEM),
            pl.BlockSpec(memory_space=pltpu.VMEM),
        ],
        out_specs=(
            pl.BlockSpec(memory_space=pltpu.VMEM),
            pl.BlockSpec(memory_space=pltpu.VMEM),
        ),
        scratch_shapes=[
            pltpu.VMEM((NT, M, S), jnp.bfloat16),
            pltpu.VMEM((C, E, K, S, S), jnp.bfloat16),
            pltpu.VMEM((2, tall, half), jnp.float32),
            pltpu.VMEM((tall, half), jnp.float32),
            pltpu.VMEM((R - 1, tall // R, half), jnp.float32),
            pltpu.VMEM((Z - 1, tall // R // Z, half), jnp.float32),
            pltpu.VMEM((2, tall, half), jnp.float32),
            dma((1 + TPD,)), dma((C, TPD)), dma((C, TPD)),
            dma((Z,)), dma((Z,)), dma((Z,)),
            dma((Z, R)), dma((Z, R)), dma((Z, R)), dma((Z, R)), dma, dma,
            dma, dma, dma((R - 1,)), dma((R - 1,)), dma((Z - 1,)), dma((Z - 1,)),
            dma((Z - 1,)), dma((Z - 1,)), dma((R - 1,)), dma((R - 1,)), dma((R,)), dma((R,)),
        ],
        compiler_params=pltpu.CompilerParams(
            collective_id=0, has_side_effects=True, vmem_limit_bytes=56 * 1024 * 1024
        ),
    )(ancestor_inv, factor, struct, validity, diag_inverse)
    return column_block, diagonal


def solution(mesh):
    return jax.shard_map(
        functools.partial(body, mesh.shape["rows"], mesh.shape["cols"]),
        mesh=mesh,
        in_specs=(P("rows", "cols"), P("cols", None, None, None), P(), P(), P()),
        out_specs=(P(("rows", "cols"), None), P()),
        check_vma=False,
    )
```

time: 310 us -> 99.2 us (0.32)
  waiting for transfers between devices: 262 us -> 0 us
  Pallas kernels: 0 us -> 93 us
  matrix products: 18.4 us -> 0 us
  between operations: 13.8 us -> 0.64 us
  local copies, waits for them, and re-layouts: 10.7 us -> 4.5 us
  other arithmetic: 4.32 us -> 0 us
    psum x1 -> x0, waiting for transfers between devices: 131 us -> none  [body(): diagonal_sum = lax.psum(partial_value, ('rows', 'cols'))]
    pallas_call x0 -> x1, Pallas kernels: none -> 93 us  [body(): pl.pallas_call(functools.partial(kernel, R, C), out_shape=(jax.ShapeDtype...]
    all_gather x1 -> x0, waiting for transfers between devices: 68.3 us -> none  [body(): shard_piece = lax.all_gather(lfactor, 'cols', axis=0, tiled=True)]
    reduce_scatter x1 -> x0, waiting for transfers between devices: 62.1 us -> none  [body(): lax.psum_scatter(-jnp.dot(block_rows, right_side, preferred_element_type=...]
    dot_general x4 -> x0, matrix products: 18.4 us -> none  [the longest x1 8.09 us: body(): jnp.einsum('kpt,pakb->takb', picker, shard_piece, preferred_element_type=...]
    convert_element_type x1 -> x0, local copies, waits for them, and re-layouts: 5.21 us -> none  [body(): col_acc = jnp.einsum('kpt,pakb->takb', picker, shard_piece, preferred_ele...]
    dynamic_slice x1 -> x0, local copies, waits for them, and re-layouts: 3.67 us -> none  [body(): slab_piece = lax.dynamic_slice_in_dim(shard_piece, offset, slab_rows, 1)]
    unnamed x6 -> x2, local copies, waits for them, and re-layouts: 1.27 us -> 4.5 us
  transfers between devices with their start and end apart: 3 -> 0, of which waited for: 3 -> 0; matrix products, arithmetic and copies ran while one was open for 3% -> 0% of each run, Pallas kernels for 0% -> 0%
where the time goes in v1:
time: 99.2 us; the launch traced here: 98.2 us
  Pallas kernels  93 us (94%)
  local copies, waits for them, and re-layouts  4.5 us (5%)
    pallas_call x1, Pallas kernels, body(): pl.pallas_call(functools.partial(kernel, R, C), out_shape=(jax.ShapeDtype...  93 us
    unnamed x2, local copies, waits for them, and re-layouts  4.5 us

profile of v1, /device:TPU:0, one launch (start us, length us, event | category | flops | bytes accessed | tf_op | source)
XLA Modules:
  0.0 98.2 jit_solution(14194691205957128643)
XLA Ops:
  0.6 93.0 %shard_map.68 = (bf16[128,1536]{1,0:T(8,128)(2,1)}, f32[6,256,256]{2,1,0:T(8,128)}) custom-call(bf16[1024,512]{1,0:T(8,128)(2,1)} %a_ref.1, bf16[1,6,256,256]{3,2,1,0:T(8,128)(2,1)} %bitcast.1, s32[6,8]{1,0:T(8,128)} %struct_ref.1, s32[6,8]{1,0:T(8,128)} %valid_ref.1, f32[6,256,256]{2,1,0:T(8,128)} %d_ref.1), custom_call_target="tpu_custom_call" | custom-call | tf_op jit(solution)/shard_map/pallas_call | solution.py:306
  93.7 1.8 %copy.9 = bf16[128,1536]{1,0:T(8,128)(2,1)} copy(bf16[128,1536]{1,0:T(8,128)(2,1)} %get-tuple-element.4) | data formatting | bytes 786432
  95.5 2.7 %copy.10 = f32[6,256,256]{2,1,0:T(8,128)} copy(f32[6,256,256]{2,1,0:T(8,128)} %get-tuple-element.5) | data formatting | bytes 3145728

commit v2 on v1

v2 whole, which is shorter than its diff:
```python
import functools

import jax
import jax.numpy as jnp
from jax import lax
from jax.experimental import pallas as pl
from jax.experimental.pallas import tpu as pltpu
from jax.sharding import PartitionSpec as P

MESH = pl.DeviceIdType.MESH
GROUPS = 3


def kernel(
    R, C, a_ref, l_ref, struct_ref, valid_ref, col_ref, f,
    abuf, tiles, lbuf, q, x1, x2, x3,
    loc_sem, a_send, a_recv,
    lz_send_up, lz_send_dn, lz_recv, lp_send, lp_recv, lh_send, lh_recv, lc_send, lc_recv, lo_send, lo_recv,
    d1_send, d1_recv, d2_send, d2_recv, d3_send, d3_recv,
    d4_send, d4_recv, d5_send, d5_recv, d6_send, d6_recv,
):
    Z = C // 2
    r = lax.axis_index("rows")
    c = lax.axis_index("cols")
    z = c // 2
    core = c % 2
    sib = z * 2 + 1 - core
    E, K, S = l_ref.shape[0], l_ref.shape[1], l_ref.shape[2]
    NP = C * E
    TPD = a_ref.shape[1] // S
    M = a_ref.shape[0] // C
    piece = S // R
    G = q.shape[1]
    KG = K // G

    def wrap(v, n):
        return lax.rem(v, n)

    barrier = pltpu.get_barrier_semaphore()
    for d in range(1, C):
        pl.semaphore_signal(barrier, inc=1, device_id=(r, wrap(c + d, C)), device_id_type=MESH)
    for d in range(1, R):
        pl.semaphore_signal(barrier, inc=1, device_id=(wrap(r + d, R), c), device_id_type=MESH)
    pl.semaphore_wait(barrier, C - 1 + R - 1)

    def remote(src, dst, ssem, rsem, dev):
        return pltpu.make_async_remote_copy(
            src_ref=src, dst_ref=dst, send_sem=ssem, recv_sem=rsem,
            device_id=dev, device_id_type=MESH,
        )

    def entry(zz):
        return zz * 2 + core

    def rows_of(rr):
        return pl.ds(pl.multiple_of(rr * piece, piece), piece)

    def own_z(zn, ssem):
        return remote(
            l_ref.at[:, :, rows_of(r), :], lbuf.at[c, :, :, rows_of(r), :],
            ssem, lz_recv.at[z], (r, entry(zn)),
        )

    @pl.when(z + 1 < Z)
    def _():
        own_z(z + 1, lz_send_up.at[z]).start()

    @pl.when(z > 0)
    def _():
        own_z(z - 1, lz_send_dn.at[z]).start()

    own_core = remote(l_ref, lbuf.at[c], lo_send, lo_recv, (r, sib))
    own_core.start()
    own_l = pltpu.make_async_copy(l_ref, lbuf.at[c], loc_sem.at[0])
    own_l.start()

    def a_copy(d):
        cn = wrap(c + d, C)
        return remote(
            a_ref.at[pl.ds(pl.multiple_of(cn * M, M), M), :],
            abuf.at[c], a_send.at[d], a_recv.at[d], (r, cn),
        )

    own_a = pltpu.make_async_copy(
        a_ref.at[pl.ds(pl.multiple_of(c * M, M), M), :], abuf.at[c], loc_sem.at[1]
    )
    own_a.start()

    def fwd_z(zz, zn, ssem):
        ref = lbuf.at[entry(zz), :, :, rows_of(r), :]
        return remote(ref, ref, ssem, lz_recv.at[zz], (r, entry(zn)))

    def plane(zz, rr, rn):
        ref = lbuf.at[entry(zz), :, :, rows_of(rr), :]
        return remote(ref, ref, lp_send.at[zz, rn], lp_recv.at[zz, rr], (rn, c))

    def across(zz, rr):
        ref = lbuf.at[entry(zz), :, :, rows_of(rr), :]
        return remote(ref, ref, lc_send.at[zz, rr], lc_recv.at[zz, rr], (r, sib))

    def across_in(zz, rr):
        ref = lbuf.at[zz * 2 + 1 - core, :, :, rows_of(rr), :]
        return remote(ref, ref, lc_send.at[zz, rr], lc_recv.at[zz, rr], (r, sib))

    square = R == 4
    near = [r + 1 - 2 * lax.rem(r, 2), wrap(r + 2, R)] if square else []
    part_rows = piece // 2

    def half_ref(zz, rr, h):
        at = pl.ds(pl.multiple_of(rr * piece + h * part_rows, part_rows), part_rows)
        return lbuf.at[entry(zz), :, :, at, :]

    def corner(zz, rr, h, rn):
        ref = half_ref(zz, rr, h)
        return remote(ref, ref, lh_send.at[zz, h], lh_recv.at[zz, h], (rn, c))

    targets = near if square else [wrap(r + d, R) for d in range(1, R)]

    def arrived(zz):
        for rn in targets:
            plane(zz, r, rn).start()
        across(zz, r).start()

    def send_slabs():
        for d in sorted(range(1, C), key=lambda d: abs(d - C // 2)):
            a_copy(d).start()

    for s in range(1, Z):
        if s == Z - 1:
            send_slabs()
        @pl.when(z - s >= 0)
        def _():
            fwd_z(z - s, z, lz_send_up.at[z - s]).wait_recv()

            @pl.when(z + 1 < Z)
            def _():
                fwd_z(z - s, z + 1, lz_send_up.at[z - s]).start()
            arrived(z - s)

        @pl.when(z + s < Z)
        def _():
            fwd_z(z + s, z, lz_send_dn.at[z + s]).wait_recv()

            @pl.when(z > 0)
            def _():
                fwd_z(z + s, z - 1, lz_send_dn.at[z + s]).start()
            arrived(z + s)

    for s in range(1, Z):
        zz = wrap(z + s, Z)
        for i, rr in enumerate(targets):
            plane(zz, rr, r).wait_recv()
            if square:
                corner(zz, rr, i, near[1 - i]).start()
            across(zz, rr).start()
    if square:
        far = near[0] + near[1] - r
        for s in range(1, Z):
            zz = wrap(z + s, Z)
            for h in range(2):
                corner(zz, far, h, r).wait_recv()
            across(zz, far).start()

    own_l.wait()
    remote(l_ref, lbuf.at[sib], lo_send, lo_recv, (r, sib)).wait_recv()
    def cut_tiles(cs):
        for j in range(TPD):
            tiles[cs * TPD + j] = abuf[cs, :, j * S : (j + 1) * S]

    own_a.wait()
    cut_tiles(c)
    for d in range(1, C):
        cs = wrap(c + C - d, C)
        remote(abuf.at[cs], abuf.at[cs], a_send.at[d], a_recv.at[d], (r, cs)).wait_recv()
        cut_tiles(cs)
    for s in range(1, Z):
        for d in range(R):
            across_in(wrap(z + s, Z), wrap(r + d, R)).wait_recv()

    start_row = r * (C * M) + c * M
    own_tile = start_row // S
    offset = pl.multiple_of(start_row % S, M)

    def one_node(g, k, carry):
        acc = jnp.zeros((M, S), jnp.float32)
        present = jnp.int32(0)
        which = jnp.int32(0)
        for p in range(NP):
            t = struct_ref[k, p]
            ok = valid_ref[k, p] > 0
            hit = jnp.where(ok & (t == own_tile), 1, 0)
            present = present + hit
            which = which + hit * p
            term = jnp.dot(
                tiles[t],
                lbuf[p // E, p % E, k],
                preferred_element_type=jnp.float32,
            )
            acc = acc + term * jnp.where(ok, 1.0, 0.0)
        here = present.astype(jnp.float32)
        col_ref[:, pl.ds(pl.multiple_of(k * S, S), S)] = (acc * (-here)).astype(jnp.bfloat16)
        panel = lbuf[which // E, which % E, k, pl.ds(offset, M), :] * here.astype(jnp.bfloat16)
        hi = acc.astype(jnp.bfloat16)
        lo = (acc - hi.astype(jnp.float32)).astype(jnp.bfloat16)
        out = lax.dot_general(
            jnp.concatenate([panel, panel], axis=0), jnp.concatenate([hi, lo], axis=0),
            (((0,), (0,)), ((), ())), preferred_element_type=jnp.float32,
        )
        at = pl.ds(pl.multiple_of((k - g * KG) * S, S), S)
        q[0, g, at, :] = out[:, : S // 2]
        q[1, g, at, :] = out[:, S // 2 :]
        return carry

    n_r = (KG * S) // R
    n_z = n_r // Z
    sends = []

    def at_r(rr):
        return pl.ds(pl.multiple_of(rr * n_r, n_r), n_r)

    def at_z(rr, zz):
        return pl.ds(pl.multiple_of(rr * n_r + zz * n_z, n_z), n_z)

    def launch(*args):
        cp = remote(*args)
        cp.start()
        sends.append(cp)

    def landed(ref, ssem, rsem):
        remote(ref, ref, ssem, rsem, (r, sib)).wait_recv()

    def multiply(g):
        lax.fori_loop(g * KG, (g + 1) * KG, functools.partial(one_node, g), 0)
        launch(q.at[1 - core, g], x1.at[g], d1_send.at[g], d1_recv.at[g], (r, sib))

    def add_core(g):
        landed(x1.at[g], d1_send.at[g], d1_recv.at[g])
        x1[g] = x1[g] + q[core, g]
        for d in range(1, R):
            rn = wrap(r + d, R)
            launch(
                x1.at[g, at_r(rn)], x2.at[g, d - 1],
                d2_send.at[g, d - 1], d2_recv.at[g, d - 1], (rn, c),
            )

    def add_plane(g):
        part = x1[g, at_r(r), :]
        for d in range(1, R):
            landed(x2.at[g, d - 1], d2_send.at[g, d - 1], d2_recv.at[g, d - 1])
            part = part + x2[g, d - 1]
        q[core, g, at_r(0), :] = part
        for s in range(1, Z):
            zn = wrap(z + s, Z)
            launch(
                q.at[core, g, at_z(0, zn)], x3.at[g, s - 1],
                d3_send.at[g, s - 1], d3_recv.at[g, s - 1], (r, entry(zn)),
            )

    def add_z(g):
        part = q[core, g, at_z(0, z), :]
        for s in range(1, Z):
            landed(x3.at[g, s - 1], d3_send.at[g, s - 1], d3_recv.at[g, s - 1])
            part = part + x3[g, s - 1]
        f[core, g, at_z(r, z), :] = part
        ref = f.at[core, g, at_z(r, z)]
        for s in range(1, Z):
            launch(
                ref, ref, d4_send.at[g, s - 1], d4_recv.at[g, s - 1],
                (r, entry(wrap(z + s, Z))),
            )

    def spread_plane(g):
        for s in range(1, Z):
            ref = f.at[core, g, at_z(r, wrap(z + Z - s, Z))]
            landed(ref, d4_send.at[g, s - 1], d4_recv.at[g, s - 1])
        ref = f.at[core, g, at_r(r)]
        for d in range(1, R):
            launch(
                ref, ref, d5_send.at[g, d - 1], d5_recv.at[g, d - 1], (wrap(r + d, R), c)
            )
        launch(ref, ref, d6_send.at[g, 0], d6_recv.at[g, 0], (r, sib))

    def spread_core(g):
        for d in range(1, R):
            ref = f.at[core, g, at_r(wrap(r + R - d, R))]
            landed(ref, d5_send.at[g, d - 1], d5_recv.at[g, d - 1])
            launch(ref, ref, d6_send.at[g, d], d6_recv.at[g, d], (r, sib))

    def store(g):
        for d in range(R):
            ref = f.at[1 - core, g, at_r(wrap(r + R - d, R))]
            landed(ref, d6_send.at[g, d], d6_recv.at[g, d])

    stages = [multiply, add_core, add_plane, add_z, spread_plane, spread_core, store]
    for step in range(len(stages) + G - 1):
        for g in range(G):
            if 0 <= step - g < len(stages):
                stages[step - g](g)

    @pl.when(z + 1 < Z)
    def _():
        own_z(z + 1, lz_send_up.at[z]).wait_send()

    @pl.when(z > 0)
    def _():
        own_z(z - 1, lz_send_dn.at[z]).wait_send()

    own_core.wait_send()
    for d in range(1, C):
        a_copy(d).wait_send()

    def sent(zz):
        for rn in targets:
            plane(zz, r, rn).wait_send()
        across(zz, r).wait_send()

    for s in range(1, Z):
        @pl.when(z - s >= 0)
        def _():
            @pl.when(z + 1 < Z)
            def _():
                fwd_z(z - s, z + 1, lz_send_up.at[z - s]).wait_send()
            sent(z - s)

        @pl.when(z + s < Z)
        def _():
            @pl.when(z > 0)
            def _():
                fwd_z(z + s, z - 1, lz_send_dn.at[z + s]).wait_send()
            sent(z + s)

    for s in range(1, Z):
        zz = wrap(z + s, Z)
        for d in range(1, R):
            across(zz, wrap(r + d, R)).wait_send()
        if square:
            for h in range(2):
                corner(zz, near[h], h, near[1 - h]).wait_send()
    for cp in sends:
        cp.wait_send()


def body(R, C, ancestor_inv, lfactor, struct, validity, diag_inverse):
    E, S, K, _ = lfactor.shape
    Z = C // 2
    rows, width = ancestor_inv.shape
    M = rows // C
    G = GROUPS if K % GROUPS == 0 else 1
    tall = K // G * S
    half = S // 2
    factor = jnp.transpose(lfactor, (0, 2, 1, 3))
    dma = pltpu.SemaphoreType.DMA
    column_block, sums = pl.pallas_call(
        functools.partial(kernel, R, C),
        out_shape=(
            jax.ShapeDtypeStruct((M, K * S), jnp.bfloat16),
            jax.ShapeDtypeStruct((2, G, tall, half), jnp.float32),
        ),
        in_specs=[
            pl.BlockSpec(memory_space=pl.ANY),
            pl.BlockSpec(memory_space=pl.ANY),
            pl.BlockSpec(memory_space=pltpu.SMEM),
            pl.BlockSpec(memory_space=pltpu.SMEM),
        ],
        out_specs=(
            pl.BlockSpec(memory_space=pltpu.VMEM),
            pl.BlockSpec(memory_space=pltpu.VMEM),
        ),
        scratch_shapes=[
            pltpu.VMEM((C, M, width), jnp.bfloat16),
            pltpu.VMEM((C * (width // S), M, S), jnp.bfloat16),
            pltpu.VMEM((C, E, K, S, S), jnp.bfloat16),
            pltpu.VMEM((2, G, tall, half), jnp.float32),
            pltpu.VMEM((G, tall, half), jnp.float32),
            pltpu.VMEM((G, R - 1, tall // R, half), jnp.float32),
            pltpu.VMEM((G, Z - 1, tall // R // Z, half), jnp.float32),
            dma((2,)), dma((C,)), dma((C,)),
            dma((Z,)), dma((Z,)), dma((Z,)),
            dma((Z, R)), dma((Z, R)), dma((Z, 2)), dma((Z, 2)), dma((Z, R)), dma((Z, R)), dma, dma,
            dma((G,)), dma((G,)), dma((G, R - 1)), dma((G, R - 1)), dma((G, Z - 1)), dma((G, Z - 1)),
            dma((G, Z - 1)), dma((G, Z - 1)), dma((G, R - 1)), dma((G, R - 1)), dma((G, R)), dma((G, R)),
        ],
        compiler_params=pltpu.CompilerParams(
            collective_id=0, has_side_effects=True, vmem_limit_bytes=56 * 1024 * 1024
        ),
    )(ancestor_inv, factor, struct, validity)
    sums = jnp.concatenate([sums[0], sums[1]], axis=-1).reshape(K, S, S)
    return column_block, diag_inverse + sums


def solution(mesh):
    return jax.shard_map(
        functools.partial(body, mesh.shape["rows"], mesh.shape["cols"]),
        mesh=mesh,
        in_specs=(P("rows", "cols"), P("cols", None, None, None), P(), P(), P()),
        out_specs=(P(("rows", "cols"), None), P()),
        check_vma=False,
    )
```

time: 99.2 us -> 78.8 us (0.79)
  Pallas kernels: 93 us -> 73.9 us
  local copies, waits for them, and re-layouts: 4.5 us -> 2.62 us
  other arithmetic: 0 us -> 1.3 us
    pallas_call x1, Pallas kernels: 93 us -> 73.9 us  [body(): pl.pallas_call(functools.partial(kernel, R, C), out_shape=(jax.ShapeDtype...]
    unnamed x2 -> x5, local copies, waits for them, and re-layouts: 4.5 us -> 1.03 us
    slice x0 -> x1, local copies, waits for them, and re-layouts: none -> 1.59 us  [body(): sums = jnp.concatenate([sums[0], sums[1]], axis=-1).reshape(K, S, S)]
    add x0 -> x1, other arithmetic: none -> 1.3 us  [body(): return (column_block, diag_inverse + sums)]
where the time goes in v2:
time: 78.8 us; the launch traced here: 78.5 us
  Pallas kernels  73.9 us (94%)
  local copies, waits for them, and re-layouts  2.62 us (3%)
  other arithmetic  1.3 us (2%)
    pallas_call x1, Pallas kernels, body(): pl.pallas_call(functools.partial(kernel, R, C), out_shape=(jax.ShapeDtype...  73.9 us
    slice x1, local copies, waits for them, and re-layouts, body(): sums = jnp.concatenate([sums[0], sums[1]], axis=-1).reshape(K, S, S)  1.59 us

profile of v2, /device:TPU:0, one launch (start us, length us, event | category | flops | bytes accessed | tf_op | source)
XLA Modules:
  0.0 78.5 jit_solution(8612438159988911123)
XLA Ops:
  0.6 73.9 %shard_map.68 = (bf16[128,1536]{1,0:T(8,128)(2,1)}, f32[2,3,512,128]{3,2,1,0:T(8,128)}) custom-call(bf16[1024,512]{1,0:T(8,128)(2,1)} %a_ref.1, bf16[1,6,256,256]{3,2,1,0:T(8,128)(2,1)} %bitcast.5, s32[6,8]{1,0:T(8,128)} %struct_ref.1, s32[6,8]{1,0:T(8,128)} %valid_ref.1), custom_call_target="tpu_custom_call" | custom-call | tf_op jit(solution)/shard_map/pallas_call | solution.py:353
  74.6 0.0 copy-start
  74.6 1.6 %fusion = (f32[1,3,512,128]{3,2,1,0:T(8,128)S(1)}, f32[1,3,512,128]{3,2,1,0:T(8,128)S(1)}) fusion(f32[2,3,512,128]{3,2,1,0:T(8,128)} %get-tuple-element.5), kind=kLoop, calls=%fused_computation.1 | loop fusion | bytes 3145728 | tf_op jit(solution)/shard_map/slice | solution.py:387
  76.2 0.3 copy-done
  76.5 0.0 copy-start.1
  76.5 1.3 %maximum_add_fusion = f32[6,256,256]{2,1,0:T(8,128)} fusion(f32[6,256,256]{2,1,0:T(8,128)S(1)} %copy-done, f32[6,256,128]{2,1,0:T(8,128)S(1)} %bitcast.4, f32[6,256,128]{2,1,0:T(8,128)S(1)} %bitcast.3), kind=kLoop, calls=%fused_computation | loop fusion | flops 786432 | bytes 4718592 | tf_op jit(solution)/shard_map/add | solution.py:388
  77.8 0.0 copy-done.1
  77.8 0.7 copy.8
Async XLA Ops:
  74.6 1.9 %copy-start = (f32[6,256,256]{2,1,0:T(8,128)S(1)}, f32[6,256,256]{2,1,0:T(8,128)}, u32[]{:S(2)}) copy-start(f32[6,256,256]{2,1,0:T(8,128)} %param.9) | copy-start | bytes 4718596
  76.5 1.3 %copy-start.1 = (bf16[128,1536]{1,0:T(8,128)(2,1)S(1)}, bf16[128,1536]{1,0:T(8,128)(2,1)}, u32[]{:S(2)}) copy-start(bf16[128,1536]{1,0:T(8,128)(2,1)} %get-tuple-element.10) | copy-start | bytes 1179652
